TPU v7x, 32 devices: a whole 2x2x4 slice. The times are simulated.
32 devices in a mesh: groups: 2 (over x), row: 16 (over z, y, core).
Axes of the slice: x: 2, y: 2, z: 4, core: 2. Of those that a mesh axis runs over, the one named last changes fastest.
Arguments:
- blocks: bfloat16 [128, 14, 128, 128], P(('groups', 'row')), parts along dimension 0, may hold values from -1.2 to 1.2
- block_cols: int32 [128, 14], P('groups'), parts along dimension 0, may hold values from 0 to 63, as said below
- kept_cols: int32 [128, 14], P('groups'), parts along dimension 0, may hold values from 0 to 63, as said below
Outputs:
- square: float32 [128, 14, 128, 128], P(('groups', 'row')), parts along dimension 0
- new_blocks: float32 [128, 14, 128, 128], P(('groups', 'row')), parts along dimension 0
There are 2 independent parts, one for each index of `groups`. A program takes and returns all parts, laid end to end along the dimension named above; each array names one. Nothing has to cross between parts.
Inputs may be any that keep to these rules, and one draw needn't show every extreme that they name: `block_cols`: block row i is cell i % 4 of layer i // 4 of a periodic box of 16 layers. Slot 0 of row i holds i itself; the entries of a row are distinct cells whose layers lie within 2 of i's layer, cyclically. `kept_cols`: block row i is cell i % 4 of layer i // 4 of a periodic box of 16 layers. Slot 0 of row i holds i itself; the entries of a row are distinct cells whose layers lie within 2 of i's layer, cyclically.
All inputs are finite; a program needn't handle non-finite values.
Results may differ from a plain program's by a relative error of at most 0.0031.
Values may be sent and summed in bfloat16 or wider, within the bound.
A program may use at most 128 MiB of HBM per device.

v0:
```python
import jax
import jax.numpy as jnp
from jax import lax
from jax.sharding import PartitionSpec as P

REACH = 2


def shifted(block, axis, distance):
    devices = range(lax.axis_size(axis))
    route = [((i - distance) % len(devices), i) for i in devices]
    return lax.ppermute(block, axis, route)


def collect_blocks(blocks):
    lower_pieces = []
    moving = blocks
    for repeat in range(REACH):
        moving = shifted(moving, "row", 1)
        lower_pieces.insert(0, moving)
    upper_pieces = []
    moving = blocks
    for repeat in range(REACH):
        moving = shifted(moving, "row", -1)
        upper_pieces.append(moving)
    pieces = lower_pieces + [blocks] + upper_pieces
    return jnp.concatenate(pieces, axis=0)


def collect_factors(factor):
    lower_pieces = []
    moving = factor
    for repeat in range(REACH):
        moving = shifted(moving, "row", 1)
        lower_pieces.insert(0, moving)
    upper_pieces = []
    moving = factor
    for repeat in range(REACH):
        moving = shifted(moving, "row", -1)
        upper_pieces.append(moving)
    pieces = lower_pieces + [factor] + upper_pieces
    return jnp.concatenate(pieces, axis=0)


def multiply(own_blocks, window, row_pattern, left_cols, wanted_cols, window_base):
    block_count = row_pattern.shape[0]
    span_rows = window.shape[0]
    slot_count = window.shape[1]
    block_width = window.shape[2]
    window_ids = jnp.mod(window_base + jnp.arange(span_rows, dtype=jnp.int32), block_count)
    flattened = window.reshape(span_rows, slot_count * block_width * block_width)

    def one_row(packed):
        own_row, needed, wanted = packed
        row_pick = (needed[:, None] == window_ids[None, :]).astype(jnp.bfloat16)
        row_blocks = jnp.dot(row_pick, flattened, preferred_element_type=jnp.float32).astype(
            jnp.bfloat16
        )
        row_blocks = row_blocks.reshape(needed.shape[0], slot_count, block_width * block_width)
        pattern_rows = row_pattern[needed]
        column_pick = (pattern_rows[:, :, None] == wanted[None, None, :]).astype(jnp.bfloat16)
        picked = jnp.einsum(
            "ksw,ksf->kwf", column_pick, row_blocks, preferred_element_type=jnp.float32
        ).astype(jnp.bfloat16)
        picked = picked.reshape(needed.shape[0], wanted.shape[0], block_width, block_width)
        return jnp.einsum("kxy,kqyz->qxz", own_row, picked, preferred_element_type=jnp.float32)

    return lax.map(one_row, (own_blocks, left_cols, wanted_cols))


def local(blocks, block_cols, kept_cols):
    rows_dev = blocks.shape[0]
    block_width = blocks.shape[2]
    first_row = lax.axis_index("row") * rows_dev
    window_base = first_row - REACH * rows_dev
    local_cols = lax.dynamic_slice_in_dim(block_cols, first_row, rows_dev, 0)
    local_kept = lax.dynamic_slice_in_dim(kept_cols, first_row, rows_dev, 0)
    window_blocks = collect_blocks(blocks)
    square = multiply(blocks, window_blocks, block_cols, local_cols, local_kept, window_base)
    row_ids = first_row + jnp.arange(rows_dev, dtype=jnp.int32)
    diagonal_mask = (local_kept == row_ids[:, None]).astype(jnp.float32)
    identity_block = jnp.eye(block_width, dtype=jnp.float32)
    factor = (3.0 * diagonal_mask[:, :, None, None] * identity_block - square).astype(jnp.bfloat16)
    window_factors = collect_factors(factor)
    new_blocks = 0.5 * multiply(
        blocks, window_factors, kept_cols, local_cols, local_cols, window_base
    )
    return (square, new_blocks)


def solution(mesh):
    in_specs = (P(("groups", "row"), None, None, None), P("groups", None), P("groups", None))
    out_specs = (P(("groups", "row"), None, None, None), P(("groups", "row"), None, None, None))
    return jax.shard_map(local, mesh=mesh, in_specs=in_specs, out_specs=out_specs, check_vma=False)
```

profile of v0, /device:TPU:1, one launch (start us, length us, event | category | flops | bytes accessed | tf_op | source)
XLA Modules:
  0.0 628.2 jit_solution(232350374819681336)
XLA Ops:
  0.6 2.7 collective-permute-start
  3.3 40.1 %collective-permute-done = bf16[4,14,128,128]{3,2,1,0:T(8,128)(2,1)} collective-permute-done((bf16[4,14,128,128]{3,2,1,0:T(8,128)(2,1)}, bf16[4,14,128,128]{3,2,1,0:T(8,128)(2,1)}, u32[]{:S(2)}, u32[]{:S(2)}) %collective-permute-start) | collective-permute-done | bytes 1835040 | tf_op jit(solution)/shard_map/ppermute | solution.py:12
  45.9 19.6 %collective-permute-done.2 = bf16[4,14,128,128]{3,2,1,0:T(8,128)(2,1)S(1)} collective-permute-done((bf16[4,14,128,128]{3,2,1,0:T(8,128)(2,1)}, bf16[4,14,128,128]{3,2,1,0:T(8,128)(2,1)S(1)}, u32[]{:S(2)}, u32[]{:S(2)}) %collective-permute-start.2) | collective-permute-done | bytes 1835040 | tf_op jit(solution)/shard_map/ppermute | solution.py:12
  67.2 17.9 %collective-permute-done.1 = bf16[4,14,128,128]{3,2,1,0:T(8,128)(2,1)} collective-permute-done((bf16[4,14,128,128]{3,2,1,0:T(8,128)(2,1)}, bf16[4,14,128,128]{3,2,1,0:T(8,128)(2,1)}, u32[]{:S(2)}, u32[]{:S(2)}) %collective-permute-start.1) | collective-permute-done | bytes 1835040 | tf_op jit(solution)/shard_map/ppermute | solution.py:12
  85.1 3.0 constant_dynamic-update-slice_fusion.5
  88.1 3.0 constant_dynamic-update-slice_fusion.4
  91.1 3.0 constant_dynamic-update-slice_fusion.3
  95.4 3.0 constant_dynamic-update-slice_fusion.1
  98.4 8.8 %pad.2 = bf16[24,1792,128]{2,1,0:T(8,128)(2,1)} pad(bf16[20,1792,128]{2,1,0:T(8,128)(2,1)} %bitcast.25, bf16[]{:T(256)} %constant.74), padding=0_4x0_0x0_0 | pad | bytes 20185090
  107.2 16.4 %copy.20 = bf16[3,8,1792,128]{3,1,2,0:T(8,128)(2,1)} copy(bf16[3,8,1792,128]{3,2,1,0:T(8,128)(2,1)} %bitcast.89) | data formatting | bytes 22020096
  123.6 181.4 %while.22 = (s32[]{:T(128)}, f32[4,14,128,128]{2,3,1,0:T(8,128)}, s32[4,14]{1,0:T(4,128)S(1)}, s32[64,14]{1,0:T(8,128)S(1)}, s32[4,14]{1,0:T(4,128)S(1)}, /*inde...) while((s32[]{:T(128)}, f32[4,14,128,128]{2,3,1,0:T(8,128)}, ...), condition=%wide.region_1.2_spmd.clone, body=%wide.region_0.1_spmd.clone.sunk | while | flops 1046876416 | bytes 61939816 | solution.py:68
  123.8 9.4 %convolution_convert_fusion.8 = bf16[14,229376]{1,0:T(8,128)(2,1)} fusion(bf16[20,229376]{1,0:T(8,128)(2,1)} %get-tuple-element.289, s32[20]{0:T(128)S(1)} %and_select_fusion.4, s32[14]{0:T(128)S(1)} %get-tuple-element.257), kind=kOutput, calls=%fused_computation.4.clone.1 | convolution fusion | flops 131662104 | bytes 15597704 | tf_op jit(solution)/shard_map/while/body/eval_jaxpr/dot_general | solution.py:56
  133.2 11.1 %reshape.146 = bf16[14,14,16384]{2,1,0:T(8,128)(2,1)} reshape(bf16[14,229376]{1,0:T(8,128)(2,1)} %convolution_convert_fusion.8) | data formatting | bytes 12845056 | tf_op jit(solution)/shard_map/while/body/eval_jaxpr/reshape | solution.py:59
  144.9 8.2 %convolution_convert_fusion.9 = bf16[14,14,16384]{2,1,0:T(8,128)(2,1)} fusion(bf16[14,14,16384]{2,1,0:T(8,128)(2,1)} %reshape.146, s32[14,14]{1,0:T(8,128)S(1)} %gather_fusion, s32[14]{0:T(128)S(1)} %get-tuple-element.258), kind=kOutput, calls=%fused_computation.5.clone.1 | convolution fusion | flops 93129400 | bytes 12845896 | tf_op jit(solution)/shard_map/while/body/eval_jaxpr/ksw,ksf->kwf/dot_general | solution.py:62
  153.1 10.3 %reshape.147 = bf16[14,14,128,128]{3,2,1,0:T(8,128)(2,1)} reshape(bf16[14,14,16384]{2,1,0:T(8,128)(2,1)} %convolution_convert_fusion.9) | data formatting | bytes 12845056 | tf_op jit(solution)/shard_map/while/body/eval_jaxpr/reshape | solution.py:65
  163.4 5.7 fusion.62
  169.1 9.4 %convolution_convert_fusion.8 = bf16[14,229376]{1,0:T(8,128)(2,1)} fusion(bf16[20,229376]{1,0:T(8,128)(2,1)} %get-tuple-element.289, s32[20]{0:T(128)S(1)} %and_select_fusion.4, s32[14]{0:T(128)S(1)} %get-tuple-element.257), kind=kOutput, calls=%fused_computation.4.clone.1 | convolution fusion | flops 131662104 | bytes 15597704 | tf_op jit(solution)/shard_map/while/body/eval_jaxpr/dot_general | solution.py:56
  178.5 11.1 %reshape.146 = bf16[14,14,16384]{2,1,0:T(8,128)(2,1)} reshape(bf16[14,229376]{1,0:T(8,128)(2,1)} %convolution_convert_fusion.8) | data formatting | bytes 12845056 | tf_op jit(solution)/shard_map/while/body/eval_jaxpr/reshape | solution.py:59
  190.1 8.2 %convolution_convert_fusion.9 = bf16[14,14,16384]{2,1,0:T(8,128)(2,1)} fusion(bf16[14,14,16384]{2,1,0:T(8,128)(2,1)} %reshape.146, s32[14,14]{1,0:T(8,128)S(1)} %gather_fusion, s32[14]{0:T(128)S(1)} %get-tuple-element.258), kind=kOutput, calls=%fused_computation.5.clone.1 | convolution fusion | flops 93129400 | bytes 12845896 | tf_op jit(solution)/shard_map/while/body/eval_jaxpr/ksw,ksf->kwf/dot_general | solution.py:62
  198.3 10.3 %reshape.147 = bf16[14,14,128,128]{3,2,1,0:T(8,128)(2,1)} reshape(bf16[14,14,16384]{2,1,0:T(8,128)(2,1)} %convolution_convert_fusion.9) | data formatting | bytes 12845056 | tf_op jit(solution)/shard_map/while/body/eval_jaxpr/reshape | solution.py:65
  208.6 5.7 fusion.62
  214.3 9.4 %convolution_convert_fusion.8 = bf16[14,229376]{1,0:T(8,128)(2,1)} fusion(bf16[20,229376]{1,0:T(8,128)(2,1)} %get-tuple-element.289, s32[20]{0:T(128)S(1)} %and_select_fusion.4, s32[14]{0:T(128)S(1)} %get-tuple-element.257), kind=kOutput, calls=%fused_computation.4.clone.1 | convolution fusion | flops 131662104 | bytes 15597704 | tf_op jit(solution)/shard_map/while/body/eval_jaxpr/dot_general | solution.py:56
  223.7 11.1 %reshape.146 = bf16[14,14,16384]{2,1,0:T(8,128)(2,1)} reshape(bf16[14,229376]{1,0:T(8,128)(2,1)} %convolution_convert_fusion.8) | data formatting | bytes 12845056 | tf_op jit(solution)/shard_map/while/body/eval_jaxpr/reshape | solution.py:59
  235.3 8.2 %convolution_convert_fusion.9 = bf16[14,14,16384]{2,1,0:T(8,128)(2,1)} fusion(bf16[14,14,16384]{2,1,0:T(8,128)(2,1)} %reshape.146, s32[14,14]{1,0:T(8,128)S(1)} %gather_fusion, s32[14]{0:T(128)S(1)} %get-tuple-element.258), kind=kOutput, calls=%fused_computation.5.clone.1 | convolution fusion | flops 93129400 | bytes 12845896 | tf_op jit(solution)/shard_map/while/body/eval_jaxpr/ksw,ksf->kwf/dot_general | solution.py:62
  243.5 10.3 %reshape.147 = bf16[14,14,128,128]{3,2,1,0:T(8,128)(2,1)} reshape(bf16[14,14,16384]{2,1,0:T(8,128)(2,1)} %convolution_convert_fusion.9) | data formatting | bytes 12845056 | tf_op jit(solution)/shard_map/while/body/eval_jaxpr/reshape | solution.py:65
  253.8 5.7 fusion.62
  259.5 9.4 %convolution_convert_fusion.8 = bf16[14,229376]{1,0:T(8,128)(2,1)} fusion(bf16[20,229376]{1,0:T(8,128)(2,1)} %get-tuple-element.289, s32[20]{0:T(128)S(1)} %and_select_fusion.4, s32[14]{0:T(128)S(1)} %get-tuple-element.257), kind=kOutput, calls=%fused_computation.4.clone.1 | convolution fusion | flops 131662104 | bytes 15597704 | tf_op jit(solution)/shard_map/while/body/eval_jaxpr/dot_general | solution.py:56
  268.9 11.1 %reshape.146 = bf16[14,14,16384]{2,1,0:T(8,128)(2,1)} reshape(bf16[14,229376]{1,0:T(8,128)(2,1)} %convolution_convert_fusion.8) | data formatting | bytes 12845056 | tf_op jit(solution)/shard_map/while/body/eval_jaxpr/reshape | solution.py:59
  280.5 8.2 %convolution_convert_fusion.9 = bf16[14,14,16384]{2,1,0:T(8,128)(2,1)} fusion(bf16[14,14,16384]{2,1,0:T(8,128)(2,1)} %reshape.146, s32[14,14]{1,0:T(8,128)S(1)} %gather_fusion, s32[14]{0:T(128)S(1)} %get-tuple-element.258), kind=kOutput, calls=%fused_computation.5.clone.1 | convolution fusion | flops 93129400 | bytes 12845896 | tf_op jit(solution)/shard_map/while/body/eval_jaxpr/ksw,ksf->kwf/dot_general | solution.py:62
  288.7 10.3 %reshape.147 = bf16[14,14,128,128]{3,2,1,0:T(8,128)(2,1)} reshape(bf16[14,14,16384]{2,1,0:T(8,128)(2,1)} %convolution_convert_fusion.9) | data formatting | bytes 12845056 | tf_op jit(solution)/shard_map/while/body/eval_jaxpr/reshape | solution.py:65
  299.0 5.7 fusion.62
  307.6 2.5 collective-permute-start.4
  310.1 39.1 %collective-permute-done.4 = bf16[4,14,128,128]{2,3,1,0:T(8,128)(2,1)} collective-permute-done((bf16[4,14,128,128]{2,3,1,0:T(8,128)(2,1)S(1)}, bf16[4,14,128,128]{2,3,1,0:T(8,128)(2,1)}, u32[]{:S(2)}, u32[]{:S(2)}) %collective-permute-start.4) | collective-permute-done | bytes 1835040 | tf_op jit(solution)/shard_map/ppermute | solution.py:12
  349.2 2.6 collective-permute-start.5
  352.5 5.1 copy.13
  357.6 33.3 %collective-permute-done.5 = bf16[4,14,128,128]{2,3,1,0:T(8,128)(2,1)} collective-permute-done((bf16[4,14,128,128]{2,3,1,0:T(8,128)(2,1)}, bf16[4,14,128,128]{2,3,1,0:T(8,128)(2,1)}, u32[]{:S(2)}, u32[]{:S(2)}) %collective-permute-start.5) | collective-permute-done | bytes 1835040 | tf_op jit(solution)/shard_map/ppermute | solution.py:12
  390.8 3.0 constant_dynamic-update-slice_fusion.10
  393.8 3.0 constant_dynamic-update-slice_fusion.9
  399.9 3.0 constant_dynamic-update-slice_fusion.6
  402.9 12.8 %copy.10 = bf16[20,14,128,128]{3,2,1,0:T(8,128)(2,1)} copy(bf16[20,14,128,128]{2,3,1,0:T(8,128)(2,1)} %constant_dynamic-update-slice_fusion.6) | data formatting | bytes 18350080 | tf_op jit(solution)/shard_map/concatenate | solution.py:42
  415.8 8.8 %pad.3 = bf16[24,1792,128]{2,1,0:T(8,128)(2,1)} pad(bf16[20,1792,128]{2,1,0:T(8,128)(2,1)} %bitcast.90, bf16[]{:T(256)} %constant.74), padding=0_4x0_0x0_0 | pad | bytes 20185090
  424.6 16.4 %copy.21 = bf16[3,8,1792,128]{3,1,2,0:T(8,128)(2,1)} copy(bf16[3,8,1792,128]{3,2,1,0:T(8,128)(2,1)} %bitcast.88) | data formatting | bytes 22020096
  441.0 182.7 %while.23 = (s32[]{:T(128)}, f32[4,14,128,128]{3,2,1,0:T(8,128)}, s32[4,14]{1,0:T(4,128)S(1)}, s32[64,14]{1,0:T(8,128)S(1)}, bf16[20,229376]{1,0:T(8,128)(2,1)},...) while((s32[]{:T(128)}, f32[4,14,128,128]{3,2,1,0:T(8,128)}, s32[4,14]{1,0:T(4,128)S(1)}, ...), condition=%wide.region_3.4_spmd.clone, body=%wide.region_2.3_spmd.clone.sunk | while | flops 1046876416 | bytes 65609712 | solution.py:68
  441.2 9.4 %convolution_convert_fusion.10 = bf16[14,229376]{1,0:T(8,128)(2,1)} fusion(bf16[20,229376]{1,0:T(8,128)(2,1)} %get-tuple-element.313, s32[20]{0:T(128)S(1)} %and_select_fusion.5, s32[14]{0:T(128)S(1)} %fusion.69), kind=kOutput, calls=%fused_computation.28.clone.1 | convolution fusion | flops 131662104 | bytes 15597704 | tf_op jit(solution)/shard_map/while/body/eval_jaxpr/dot_general | solution.py:56
  450.6 11.1 %reshape.150 = bf16[14,14,16384]{2,1,0:T(8,128)(2,1)} reshape(bf16[14,229376]{1,0:T(8,128)(2,1)} %convolution_convert_fusion.10) | data formatting | bytes 12845056 | tf_op jit(solution)/shard_map/while/body/eval_jaxpr/reshape | solution.py:59
  462.3 8.2 %convolution_convert_fusion.11 = bf16[14,14,16384]{2,1,0:T(8,128)(2,1)} fusion(bf16[14,14,16384]{2,1,0:T(8,128)(2,1)} %reshape.150, s32[14,14]{1,0:T(8,128)S(1)} %gather_fusion.1, s32[14]{0:T(128)S(1)} %fusion.69), kind=kOutput, calls=%fused_computation.29.clone.1 | convolution fusion | flops 93129400 | bytes 12845896 | tf_op jit(solution)/shard_map/while/body/eval_jaxpr/ksw,ksf->kwf/dot_general | solution.py:62
  470.4 10.3 %reshape.151 = bf16[14,14,128,128]{3,2,1,0:T(8,128)(2,1)} reshape(bf16[14,14,16384]{2,1,0:T(8,128)(2,1)} %convolution_convert_fusion.11) | data formatting | bytes 12845056 | tf_op jit(solution)/shard_map/while/body/eval_jaxpr/reshape | solution.py:65
  480.7 4.7 convolution_bitcast_fusion.3
  486.8 9.4 %convolution_convert_fusion.10 = bf16[14,229376]{1,0:T(8,128)(2,1)} fusion(bf16[20,229376]{1,0:T(8,128)(2,1)} %get-tuple-element.313, s32[20]{0:T(128)S(1)} %and_select_fusion.5, s32[14]{0:T(128)S(1)} %fusion.69), kind=kOutput, calls=%fused_computation.28.clone.1 | convolution fusion | flops 131662104 | bytes 15597704 | tf_op jit(solution)/shard_map/while/body/eval_jaxpr/dot_general | solution.py:56
  496.2 11.1 %reshape.150 = bf16[14,14,16384]{2,1,0:T(8,128)(2,1)} reshape(bf16[14,229376]{1,0:T(8,128)(2,1)} %convolution_convert_fusion.10) | data formatting | bytes 12845056 | tf_op jit(solution)/shard_map/while/body/eval_jaxpr/reshape | solution.py:59
  507.9 8.2 %convolution_convert_fusion.11 = bf16[14,14,16384]{2,1,0:T(8,128)(2,1)} fusion(bf16[14,14,16384]{2,1,0:T(8,128)(2,1)} %reshape.150, s32[14,14]{1,0:T(8,128)S(1)} %gather_fusion.1, s32[14]{0:T(128)S(1)} %fusion.69), kind=kOutput, calls=%fused_computation.29.clone.1 | convolution fusion | flops 93129400 | bytes 12845896 | tf_op jit(solution)/shard_map/while/body/eval_jaxpr/ksw,ksf->kwf/dot_general | solution.py:62
  516.0 10.3 %reshape.151 = bf16[14,14,128,128]{3,2,1,0:T(8,128)(2,1)} reshape(bf16[14,14,16384]{2,1,0:T(8,128)(2,1)} %convolution_convert_fusion.11) | data formatting | bytes 12845056 | tf_op jit(solution)/shard_map/while/body/eval_jaxpr/reshape | solution.py:65
  526.4 4.7 convolution_bitcast_fusion.3
  532.4 9.4 %convolution_convert_fusion.10 = bf16[14,229376]{1,0:T(8,128)(2,1)} fusion(bf16[20,229376]{1,0:T(8,128)(2,1)} %get-tuple-element.313, s32[20]{0:T(128)S(1)} %and_select_fusion.5, s32[14]{0:T(128)S(1)} %fusion.69), kind=kOutput, calls=%fused_computation.28.clone.1 | convolution fusion | flops 131662104 | bytes 15597704 | tf_op jit(solution)/shard_map/while/body/eval_jaxpr/dot_general | solution.py:56
  541.8 11.1 %reshape.150 = bf16[14,14,16384]{2,1,0:T(8,128)(2,1)} reshape(bf16[14,229376]{1,0:T(8,128)(2,1)} %convolution_convert_fusion.10) | data formatting | bytes 12845056 | tf_op jit(solution)/shard_map/while/body/eval_jaxpr/reshape | solution.py:59
  553.5 8.2 %convolution_convert_fusion.11 = bf16[14,14,16384]{2,1,0:T(8,128)(2,1)} fusion(bf16[14,14,16384]{2,1,0:T(8,128)(2,1)} %reshape.150, s32[14,14]{1,0:T(8,128)S(1)} %gather_fusion.1, s32[14]{0:T(128)S(1)} %fusion.69), kind=kOutput, calls=%fused_computation.29.clone.1 | convolution fusion | flops 93129400 | bytes 12845896 | tf_op jit(solution)/shard_map/while/body/eval_jaxpr/ksw,ksf->kwf/dot_general | solution.py:62
  561.7 10.3 %reshape.151 = bf16[14,14,128,128]{3,2,1,0:T(8,128)(2,1)} reshape(bf16[14,14,16384]{2,1,0:T(8,128)(2,1)} %convolution_convert_fusion.11) | data formatting | bytes 12845056 | tf_op jit(solution)/shard_map/while/body/eval_jaxpr/reshape | solution.py:65
  572.0 4.7 convolution_bitcast_fusion.3
  578.1 9.4 %convolution_convert_fusion.10 = bf16[14,229376]{1,0:T(8,128)(2,1)} fusion(bf16[20,229376]{1,0:T(8,128)(2,1)} %get-tuple-element.313, s32[20]{0:T(128)S(1)} %and_select_fusion.5, s32[14]{0:T(128)S(1)} %fusion.69), kind=kOutput, calls=%fused_computation.28.clone.1 | convolution fusion | flops 131662104 | bytes 15597704 | tf_op jit(solution)/shard_map/while/body/eval_jaxpr/dot_general | solution.py:56
  587.5 11.1 %reshape.150 = bf16[14,14,16384]{2,1,0:T(8,128)(2,1)} reshape(bf16[14,229376]{1,0:T(8,128)(2,1)} %convolution_convert_fusion.10) | data formatting | bytes 12845056 | tf_op jit(solution)/shard_map/while/body/eval_jaxpr/reshape | solution.py:59
  599.1 8.2 %convolution_convert_fusion.11 = bf16[14,14,16384]{2,1,0:T(8,128)(2,1)} fusion(bf16[14,14,16384]{2,1,0:T(8,128)(2,1)} %reshape.150, s32[14,14]{1,0:T(8,128)S(1)} %gather_fusion.1, s32[14]{0:T(128)S(1)} %fusion.69), kind=kOutput, calls=%fused_computation.29.clone.1 | convolution fusion | flops 93129400 | bytes 12845896 | tf_op jit(solution)/shard_map/while/body/eval_jaxpr/ksw,ksf->kwf/dot_general | solution.py:62
  607.3 10.3 %reshape.151 = bf16[14,14,128,128]{3,2,1,0:T(8,128)(2,1)} reshape(bf16[14,14,16384]{2,1,0:T(8,128)(2,1)} %convolution_convert_fusion.11) | data formatting | bytes 12845056 | tf_op jit(solution)/shard_map/while/body/eval_jaxpr/reshape | solution.py:65
  617.6 4.7 convolution_bitcast_fusion.3
  623.7 4.3 broadcast_multiply_fusion
  (74 shorter events, 21.9 us)
Async XLA Ops:
  0.6 42.8 %collective-permute-start = (bf16[4,14,128,128]{3,2,1,0:T(8,128)(2,1)}, bf16[4,14,128,128]{3,2,1,0:T(8,128)(2,1)}, u32[]{:S(2)}, u32[]{:S(2)}) collective-permute-start(bf16[4,14,128,128]{3,2,1,0:T(8,128)(2,1)} %param.7), channel_id=1, source_target_pairs={{15,0},{0,1},{1,2},{2,3},{3,4},{4,5},{5,6},{6,7},{7,8},{8,9},{9,10... | collective-permute-start | bytes 5505032 | tf_op jit(solution)/shard_map/ppermute | solution.py:12
  3.3 62.2 %collective-permute-start.2 = (bf16[4,14,128,128]{3,2,1,0:T(8,128)(2,1)}, bf16[4,14,128,128]{3,2,1,0:T(8,128)(2,1)S(1)}, u32[]{:S(2)}, u32[]{:S(2)}) collective-permute-start(bf16[4,14,128,128]{3,2,1,0:T(8,128)(2,1)} %param.7), channel_id=1, source_target_pairs={{1,0},{2,1},{3,2},{4,3},{5,4},{6,5},{7,6},{8,7},{9,8},{10,9},{11,1... | collective-permute-start | bytes 5505032 | tf_op jit(solution)/shard_map/ppermute | solution.py:12
  43.5 41.6 %collective-permute-start.1 = (bf16[4,14,128,128]{3,2,1,0:T(8,128)(2,1)}, bf16[4,14,128,128]{3,2,1,0:T(8,128)(2,1)}, u32[]{:S(2)}, u32[]{:S(2)}) collective-permute-start(bf16[4,14,128,128]{3,2,1,0:T(8,128)(2,1)} %collective-permute-done), channel_id=1, source_target_pairs={{15,0},{0,1},{1,2},{2,3},{3,4},{4,5},{5,6},{6,7},{7,8},{8,9},{9,10... | collective-permute-start | bytes 5505032 | tf_op jit(solution)/shard_map/ppermute | solution.py:12
  65.5 29.9 %collective-permute-start.3 = (bf16[4,14,128,128]{3,2,1,0:T(8,128)(2,1)S(1)}, bf16[4,14,128,128]{3,2,1,0:T(8,128)(2,1)}, u32[]{:S(2)}, u32[]{:S(2)}) collective-permute-start(bf16[4,14,128,128]{3,2,1,0:T(8,128)(2,1)S(1)} %collective-permute-done.2), channel_id=1, source_target_pairs={{1,0},{2,1},{3,2},{4,3},{5,4},{6,5},{7,6},{8,7},{9,8},{10,9},{11,1... | collective-permute-start | bytes 5505032 | tf_op jit(solution)/shard_map/ppermute | solution.py:12
  66.3 29.1 %copy-start.1 = (s32[64,14]{1,0:T(8,128)}, s32[64,14]{1,0:T(8,128)S(1)}, u32[]{:S(2)}) copy-start(s32[64,14]{1,0:T(8,128)S(1)} %copy.8) | copy-start | bytes 10756
  307.6 41.6 %collective-permute-start.4 = (bf16[4,14,128,128]{2,3,1,0:T(8,128)(2,1)S(1)}, bf16[4,14,128,128]{2,3,1,0:T(8,128)(2,1)}, u32[]{:S(2)}, u32[]{:S(2)}) collective-permute-start(bf16[4,14,128,128]{2,3,1,0:T(8,128)(2,1)S(1)} %subtract_convert_fusion), channel_id=1, source_target_pairs={{15,0},{0,1},{1,2},{2,3},{3,4},{4,5},{5,6},{6,7},{7,8},{8,9},{9,10... | collective-permute-start | bytes 5505032 | tf_op jit(solution)/shard_map/ppermute | solution.py:12
  310.1 42.3 %collective-permute-start.6 = (bf16[4,14,128,128]{2,3,1,0:T(8,128)(2,1)S(1)}, bf16[4,14,128,128]{2,3,1,0:T(8,128)(2,1)S(1)}, u32[]{:S(2)}, u32[]{:S(2)}) collective-permute-start(bf16[4,14,128,128]{2,3,1,0:T(8,128)(2,1)S(1)} %subtract_convert_fusion), channel_id=1, source_target_pairs={{1,0},{2,1},{3,2},{4,3},{5,4},{6,5},{7,6},{8,7},{9,8},{10,9},{11,1... | collective-permute-start | bytes 5505032 | tf_op jit(solution)/shard_map/ppermute | solution.py:12
  349.2 41.6 %collective-permute-start.5 = (bf16[4,14,128,128]{2,3,1,0:T(8,128)(2,1)}, bf16[4,14,128,128]{2,3,1,0:T(8,128)(2,1)}, u32[]{:S(2)}, u32[]{:S(2)}) collective-permute-start(bf16[4,14,128,128]{2,3,1,0:T(8,128)(2,1)} %collective-permute-done.4), channel_id=1, source_target_pairs={{15,0},{0,1},{1,2},{2,3},{3,4},{4,5},{5,6},{6,7},{7,8},{8,9},{9,10... | collective-permute-start | bytes 5505032 | tf_op jit(solution)/shard_map/ppermute | solution.py:12
  352.4 47.5 %collective-permute-start.7 = (bf16[4,14,128,128]{2,3,1,0:T(8,128)(2,1)S(1)}, bf16[4,14,128,128]{2,3,1,0:T(8,128)(2,1)}, u32[]{:S(2)}, u32[]{:S(2)}) collective-permute-start(bf16[4,14,128,128]{2,3,1,0:T(8,128)(2,1)S(1)} %collective-permute-done.6), channel_id=1, source_target_pairs={{1,0},{2,1},{3,2},{4,3},{5,4},{6,5},{7,6},{8,7},{9,8},{10,9},{11,1... | collective-permute-start | bytes 5505032 | tf_op jit(solution)/shard_map/ppermute | solution.py:12
  357.6 39.2 %copy-start = (f32[4,14,128,128]{2,3,1,0:T(8,128)S(1)}, f32[4,14,128,128]{2,3,1,0:T(8,128)}, u32[]{:S(2)}) copy-start(f32[4,14,128,128]{2,3,1,0:T(8,128)} %get-tuple-element.134) | copy-start | bytes 11010052
  424.6 16.4 %copy-start.2 = (s32[64,14]{1,0:T(8,128)S(1)}, s32[64,14]{1,0:T(8,128)}, u32[]{:S(2)}) copy-start(s32[64,14]{1,0:T(8,128)} %copy-done.1) | copy-start | bytes 10756
where the time goes:
time: 635 us; the launch traced here: 628 us
  local copies, waits for them, and re-layouts  275 us (43%)
  matrix products  182 us (29%)
  waiting for transfers between devices  151 us (24%)
  starting transfers between devices  10.3 us (2%)
  other arithmetic  8.89 us (1%)
    ppermute x8, waiting for transfers between devices, shifted(): return lax.ppermute(block, axis, route)  151 us
    reshape x8, local copies, waits for them, and re-layouts, one_row(): row_blocks.reshape(needed.shape[0], slot_count, block_width * block_width)  88.6 us
    reshape x8, local copies, waits for them, and re-layouts, one_row(): picked.reshape(needed.shape[0], wanted.shape[0], block_width, block_width)  82.5 us
    dot_general x8, matrix products, one_row(): jnp.dot(row_pick, flattened, preferred_element_type=jnp.float32)  75.3 us
    unnamed x20, local copies, waits for them, and re-layouts  74.7 us
    dot_general x8, matrix products, one_row(): jnp.einsum('ksw,ksf->kwf', column_pick, row_blocks, preferred_element_typ...  65.3 us
    dot_general x8, matrix products, one_row(): jnp.einsum('kxy,kqyz->qxz', own_row, picked, preferred_element_type=jnp.f...  41.6 us
    concatenate x2, local copies, waits for them, and re-layouts, collect_factors(): return jnp.concatenate(pieces, axis=0)  15.9 us
  transfers between devices with their start and end apart: 8, of which 6 were waited for; matrix products, arithmetic and copies ran while one was open for 4% of the time, Pallas kernels for 0%

commit v1 on v0

v1 whole, which is shorter than its diff:
```python
import functools

import jax
import jax.numpy as jnp
from jax import lax
from jax.experimental import pallas as pl
from jax.experimental.pallas import tpu as pltpu
from jax.sharding import PartitionSpec as P

MESH = pl.DeviceIdType.MESH
LAYERS = 5
HALVES = 2


def window_layers(me, count):
    core, side = me % 2, (me // 2) % 2
    away = jnp.where(side == 0, 1, -1)
    return [
        me,
        me + 1 - 2 * core,
        (me + 2 * away + count) % count,
        (me - 2 * away + count) % count,
        (me - 1 + 2 * core + count) % count,
    ]


def tables(block_cols, kept_cols, me, count, rows):
    layers = jnp.stack(window_layers(me, count)).astype(jnp.int32)
    ids = (layers[:, None] * rows + jnp.arange(rows, dtype=jnp.int32)).reshape(-1)

    def slots(cols):
        near = cols[ids]
        match = near[:, :, None] == ids[None, None, :]
        slot = jnp.arange(cols.shape[1], dtype=jnp.int32)[None, :, None]
        return jnp.max(jnp.where(match, slot, -1), axis=1)

    def places(cols):
        own = lax.dynamic_slice_in_dim(cols, me * rows, rows, 0)
        match = own[:, :, None] == ids[None, None, :]
        place = jnp.arange(ids.shape[0], dtype=jnp.int32)
        return jnp.sum(jnp.where(match, place, 0), axis=2)

    parts = [slots(block_cols), slots(kept_cols), places(kept_cols), places(block_cols)]
    return jnp.concatenate([part.reshape(-1) for part in parts]).astype(jnp.int32)


def kernel(count, rows, slots, kept, x_ref, tab, sq_out, new_out, own_f, a, d, sq, new,
           send_sem, recv_sem, out_sem, *bufs):
    width = x_ref.shape[-1]
    span = LAYERS * rows
    pairs = rows // 2
    me = lax.axis_index("row")
    core, side = me % 2, (me // 2) % 2
    mate = me + 1 - 2 * core
    across = me + 2 - 4 * side
    onward = (me + 4 - 8 * side + count) % count
    behind = (me - 4 + 8 * side + count) % count
    shares_first = core == side

    barrier = pltpu.get_barrier_semaphore()
    for other in (mate, across, onward, behind):
        pl.semaphore_signal(barrier, inc=1, device_id={"row": other}, device_id_type=MESH)
    pl.semaphore_wait(barrier, 4)

    slots_at = (0, span * span)
    kept_at = 2 * span * span
    cols_at = kept_at + rows * kept
    depth = (slots, kept)
    pieces = rows * HALVES

    def landing(stage, source, piece):
        row, half = piece // HALVES, piece % HALVES
        length = depth[stage] // HALVES
        ref = bufs[(stage * 4 + source) * pairs + row // 2]
        return ref.at[row % 2, pl.ds(half * length, length)]

    def copy(stage, source, piece, src, device):
        return pltpu.make_async_remote_copy(
            src_ref=src,
            dst_ref=landing(stage, source, piece),
            send_sem=send_sem.at[stage, source, piece],
            recv_sem=recv_sem.at[stage, source, piece],
            device_id={"row": device},
            device_id_type=MESH,
        )

    def own_piece(stage, piece):
        row, half = piece // HALVES, piece % HALVES
        length = depth[stage] // HALVES
        ref = (x_ref, own_f)[stage]
        return ref.at[row, pl.ds(half * length, length)]

    def to_mate(stage, piece):
        return copy(stage, 0, piece, own_piece(stage, piece), mate)

    def to_across(stage, piece):
        return copy(stage, 1, piece, own_piece(stage, piece), across)

    def to_onward(stage, piece):
        return copy(stage, 2, piece, landing(stage, 1, piece), onward)

    def share(stage, piece, source):
        return copy(stage, 3, piece, landing(stage, source, piece), mate)

    def start_own(stage, row):
        for half in range(HALVES):
            to_across(stage, row * HALVES + half).start()
        for half in range(HALVES):
            to_mate(stage, row * HALVES + half).start()

    def block(ref, row, slot):
        value = ref[row, jnp.maximum(slot, 0)]
        return jnp.where(slot >= 0, value, jnp.zeros_like(value))

    def multiply(stage, source, pair):
        first = source == 0 and pair == 0
        if source == 0:
            ref, base = (x_ref, own_f)[stage], 2 * pair
        else:
            ref, base = bufs[(stage * 4 + source - 1) * pairs + pair], 0
        line = slots_at[stage] + (source * rows + 2 * pair) * span

        def body(step, carry):
            lines = []
            for row in range(2):
                at = line + row * span + 2 * step
                lines.append(jnp.concatenate(
                    [block(ref, base + row, tab[at]), block(ref, base + row, tab[at + 1])], axis=1))
            right = jnp.concatenate(lines, axis=0)
            part = jnp.dot(a[source * pairs + pair], right, preferred_element_type=jnp.float32)
            for col in range(2):
                piece = part[:, col * width:(col + 1) * width]
                if first:
                    d[2 * step + col] = piece
                else:
                    d[2 * step + col] += piece
            return carry

        lax.fori_loop(0, span // 2, body, 0)

    def gather_and_multiply(stage):
        for pair in range(pairs):
            multiply(stage, 0, pair)
        for piece in range(pieces):
            to_mate(stage, piece).wait_recv()
        for pair in range(pairs):
            multiply(stage, 1, pair)
        per_pair = 2 * HALVES
        lag = 2
        for step in range(pieces + lag):
            if step < pieces:
                to_across(stage, step).wait_recv()
                to_onward(stage, step).start()

                @pl.when(shares_first)
                def _():
                    share(stage, step, 1).start()

            late = step - lag
            if late >= 0:
                to_onward(stage, late).wait_recv()

                @pl.when(jnp.logical_not(shares_first))
                def _():
                    share(stage, late, 2).start()

            if step < pieces and (step + 1) % per_pair == 0:
                multiply(stage, 2, step // per_pair)
            if late >= 0 and (late + 1) % per_pair == 0:
                pair = late // per_pair
                multiply(stage, 3, pair)
                for piece in range(pair * per_pair, (pair + 1) * per_pair):
                    share(stage, piece, 1).wait_recv()
                multiply(stage, 4, pair)

    for row in range(rows):
        start_own(0, row)

    def build(step, carry):
        for row in range(rows):
            for col in range(2):
                slot = tab[row * span + 2 * step + col]
                a[step, row * width:(row + 1) * width, col * width:(col + 1) * width] = block(
                    x_ref, row, slot)
        return carry

    lax.fori_loop(0, LAYERS * pairs, build, 0)
    gather_and_multiply(0)

    eye = (lax.broadcasted_iota(jnp.int32, (width, width), 0)
           == lax.broadcasted_iota(jnp.int32, (width, width), 1)).astype(jnp.float32)
    for row in range(rows):
        def pick(slot, carry):
            place = tab[kept_at + row * kept + slot]
            value = d[place, row * width:(row + 1) * width, :]
            sq[row, slot] = value
            three = jnp.where(place == row, 3.0, 0.0)
            own_f[row, slot] = (three * eye - value).astype(jnp.bfloat16)
            return carry

        lax.fori_loop(0, kept, pick, 0)
        start_own(1, row)
        pltpu.make_async_copy(sq.at[row], sq_out.at[row], out_sem.at[0, row]).start()

    gather_and_multiply(1)

    for row in range(rows):
        def pick(slot, carry):
            place = tab[cols_at + row * slots + slot]
            new[row, slot] = 0.5 * d[place, row * width:(row + 1) * width, :]
            return carry

        lax.fori_loop(0, slots, pick, 0)
        pltpu.make_async_copy(new.at[row], new_out.at[row], out_sem.at[1, row]).start()

    for stage in range(2):
        for piece in range(pieces):
            to_mate(stage, piece).wait_send()
            to_across(stage, piece).wait_send()
            to_onward(stage, piece).wait_send()
            share(stage, piece, 1).wait_send()
    for row in range(rows):
        pltpu.make_async_copy(sq.at[row], sq_out.at[row], out_sem.at[0, row]).wait()
        pltpu.make_async_copy(new.at[row], new_out.at[row], out_sem.at[1, row]).wait()


def local(count, blocks, block_cols, kept_cols):
    rows, slots, width, _ = blocks.shape
    kept = kept_cols.shape[1]
    me = lax.axis_index("row")
    table = tables(block_cols, kept_cols, me, count, rows)
    span = LAYERS * rows
    pieces = rows * HALVES
    landings = [
        pltpu.VMEM((2, depth, width, width), jnp.bfloat16)
        for depth in (slots, kept)
        for _ in range(4 * (rows // 2))
    ]
    return pl.pallas_call(
        functools.partial(kernel, count, rows, slots, kept),
        out_shape=(
            jax.ShapeDtypeStruct((rows, kept, width, width), jnp.float32),
            jax.ShapeDtypeStruct((rows, slots, width, width), jnp.float32),
        ),
        in_specs=[pl.BlockSpec(memory_space=pltpu.VMEM), pl.BlockSpec(memory_space=pltpu.SMEM)],
        out_specs=(pl.BlockSpec(memory_space=pl.ANY), pl.BlockSpec(memory_space=pl.ANY)),
        scratch_shapes=[
            pltpu.VMEM((rows, kept, width, width), jnp.bfloat16),
            pltpu.VMEM((LAYERS * rows // 2, rows * width, 2 * width), jnp.bfloat16),
            pltpu.VMEM((span, rows * width, width), jnp.float32),
            pltpu.VMEM((rows, kept, width, width), jnp.float32),
            pltpu.VMEM((rows, slots, width, width), jnp.float32),
            pltpu.SemaphoreType.DMA((2, 4, pieces)),
            pltpu.SemaphoreType.DMA((2, 4, pieces)),
            pltpu.SemaphoreType.DMA((2, rows)),
        ] + landings,
        compiler_params=pltpu.CompilerParams(
            collective_id=0, has_side_effects=True, vmem_limit_bytes=48 * 1024 * 1024
        ),
    )(blocks, table)


def solution(mesh):
    count = mesh.shape["row"]
    in_specs = (P(("groups", "row"), None, None, None), P("groups", None), P("groups", None))
    out_specs = (P(("groups", "row"), None, None, None), P(("groups", "row"), None, None, None))
    return jax.shard_map(
        functools.partial(local, count), mesh=mesh, in_specs=in_specs, out_specs=out_specs,
        check_vma=False)
```

time: 635 us -> 133 us (0.21)
  local copies, waits for them, and re-layouts: 275 us -> 11 us
  matrix products: 182 us -> 0 us
  waiting for transfers between devices: 151 us -> 0 us
  Pallas kernels: 0 us -> 118 us
  starting transfers between devices: 10.3 us -> 0 us
  other arithmetic: 8.89 us -> 0.99 us
    dot_general x24 -> x0, matrix products: 182 us -> none  [the longest x8 75.3 us: one_row(): jnp.dot(row_pick, flattened, preferred_element_type=jnp.float32)]
    reshape x16 -> x4, local copies, waits for them, and re-layouts: 171 us -> 0.35 us  [tables(): part.reshape(-1)]
    ppermute x8 -> x0, waiting for transfers between devices: 151 us -> none  [shifted(): return lax.ppermute(block, axis, route)]
    pallas_call x0 -> x1, Pallas kernels: none -> 118 us  [local(): pl.pallas_call(functools.partial(kernel, count, rows, slots, kept), out_s...]
    unnamed x20 -> x8, local copies, waits for them, and re-layouts: 74.7 us -> 8.28 us
    concatenate x3 -> x0, local copies, waits for them, and re-layouts: 18.9 us -> none  [the longest x2 15.9 us: collect_factors(): return jnp.concatenate(pieces, axis=0)]
    ppermute x8 -> x0, starting transfers between devices: 10.3 us -> none  [shifted(): return lax.ppermute(block, axis, route)]
  transfers between devices with their start and end apart: 8 -> 0, of which waited for: 6 -> 0; matrix products, arithmetic and copies ran while one was open for 4% -> 0% of each run, Pallas kernels for 0% -> 0%
where the time goes in v1:
time: 133 us; the launch traced here: 131 us
  Pallas kernels  118 us (89%)
  local copies, waits for them, and re-layouts  11 us (8%)
    pallas_call x1, Pallas kernels, local(): pl.pallas_call(functools.partial(kernel, count, rows, slots, kept), out_s...  118 us
    unnamed x8, local copies, waits for them, and re-layouts  8.28 us

profile of v1, /device:TPU:1, one launch (start us, length us, event | category | flops | bytes accessed | tf_op | source)
XLA Modules:
  0.0 130.8 jit_solution(7207665040302372261)
XLA Ops:
  0.7 0.1 stack.23
  0.8 0.1 iota_add_fusion
  0.9 0.1 add.98
  1.0 0.1 add.96
  1.0 0.8 constant_dynamic-slice_fusion
  1.8 0.6 select_reduce_fusion.3
  2.5 0.1 copy.15
  2.5 0.1 reshape.108
  2.6 0.1 copy.16
  2.7 0.1 reshape.109
  2.8 0.8 copy.13
  3.6 0.6 gather_fusion
  4.2 0.8 copy.14
  5.0 0.6 gather_fusion.1
  5.5 0.2 select_reduce_fusion.1
  5.7 0.1 reshape.106
  5.8 0.1 reshape.107
  5.9 0.1 pad_add_fusion.tab
  6.0 0.0 copy-start
  6.0 1.5 %copy-done = bf16[4,14,128,128]{3,2,1,0:T(8,128)(2,1)S(1)} copy-done((bf16[4,14,128,128]{3,2,1,0:T(8,128)(2,1)S(1)}, bf16[4,14,128,128]{3,2,1,0:T(8,128)(2,1)}, u32[]{:S(2)}) %copy-start) | copy-done | bytes 1835032
  7.5 118.1 %shard_map.50 = (f32[4,14,128,128]{3,2,1,0:T(8,128)S(1)}, f32[4,14,128,128]{3,2,1,0:T(8,128)}) custom-call(bf16[4,14,128,128]{3,2,1,0:T(8,128)(2,1)S(1)} %copy-done, s32[912]{0:T(1024)S(1)} %pad_add_fusion.tab), custom_call_target="tpu_custom_call" | custom-call | tf_op jit(solution)/shard_map/pallas_call | solution.py:239
  125.6 0.0 copy-start.1
  125.6 1.9 %copy.19 = f32[4,14,128,128]{3,2,1,0:T(8,128)} copy(f32[4,14,128,128]{3,2,1,0:T(8,128)S(1)} %get-tuple-element.10) | data formatting | bytes 7340032
  127.5 1.5 %copy-done.1 = f32[4,14,128,128]{3,2,1,0:T(8,128)S(1)} copy-done((f32[4,14,128,128]{3,2,1,0:T(8,128)S(1)}, f32[4,14,128,128]{3,2,1,0:T(8,128)}, u32[]{:S(2)}) %copy-start.1) | copy-done | bytes 3670040
  129.0 1.8 %copy.20 = f32[4,14,128,128]{3,2,1,0:T(8,128)} copy(f32[4,14,128,128]{3,2,1,0:T(8,128)S(1)} %copy-done.1) | data formatting | bytes 7340032
  (3 shorter events, 0.0 us)
Async XLA Ops:
  6.0 1.5 %copy-start = (bf16[4,14,128,128]{3,2,1,0:T(8,128)(2,1)S(1)}, bf16[4,14,128,128]{3,2,1,0:T(8,128)(2,1)}, u32[]{:S(2)}) copy-start(bf16[4,14,128,128]{3,2,1,0:T(8,128)(2,1)} %x_ref.1) | copy-start | bytes 5505028
  125.6 3.4 %copy-start.1 = (f32[4,14,128,128]{3,2,1,0:T(8,128)S(1)}, f32[4,14,128,128]{3,2,1,0:T(8,128)}, u32[]{:S(2)}) copy-start(f32[4,14,128,128]{3,2,1,0:T(8,128)} %get-tuple-element.11) | copy-start | bytes 11010052

commit v2 on v1

--- a/solution.py
+++ b/solution.py
@@ -24,29 +24,38 @@
     ]
 
 
-def tables(block_cols, kept_cols, me, count, rows):
-    layers = jnp.stack(window_layers(me, count)).astype(jnp.int32)
-    ids = (layers[:, None] * rows + jnp.arange(rows, dtype=jnp.int32)).reshape(-1)
-
-    def slots(cols):
-        near = cols[ids]
-        match = near[:, :, None] == ids[None, None, :]
-        slot = jnp.arange(cols.shape[1], dtype=jnp.int32)[None, :, None]
-        return jnp.max(jnp.where(match, slot, -1), axis=1)
-
-    def places(cols):
-        own = lax.dynamic_slice_in_dim(cols, me * rows, rows, 0)
-        match = own[:, :, None] == ids[None, None, :]
-        place = jnp.arange(ids.shape[0], dtype=jnp.int32)
-        return jnp.sum(jnp.where(match, place, 0), axis=2)
-
-    parts = [slots(block_cols), slots(kept_cols), places(kept_cols), places(block_cols)]
-    return jnp.concatenate([part.reshape(-1) for part in parts]).astype(jnp.int32)
-
-
-def kernel(count, rows, slots, kept, x_ref, tab, sq_out, new_out, own_f, a, d, sq, new,
-           send_sem, recv_sem, out_sem, *bufs):
+def table_rows(span, slots, kept):
+    starts = [0]
+    for length in (span, span, kept, slots):
+        starts.append(starts[-1] + (length + 7) // 8 * 8)
+    return starts
+
+
+def fill_tables(cols_ref, kept_ref, out, layers, rows, starts):
+    span = LAYERS * rows
+    line = lax.broadcasted_iota(jnp.int32, (span, cols_ref.shape[1]), 0)
+    ids = jnp.zeros_like(line)
+    for index, layer in enumerate(layers):
+        ids = jnp.where(line // rows == index, layer * rows + line % rows, ids)
+    for start, ref in zip(starts[:2], (cols_ref, kept_ref)):
+        found = jnp.full_like(ids, -1)
+        for slot in range(ref.shape[0]):
+            found = jnp.where(ref[slot:slot + 1, :] == ids, slot, found)
+        out[start:start + span, :] = found
+    for start, ref in zip(starts[2:4], (kept_ref, cols_ref)):
+        cols = ref[...]
+        place = jnp.zeros_like(cols)
+        for index, layer in enumerate(layers):
+            for row in range(rows):
+                place = jnp.where(cols == layer * rows + row, index * rows + row, place)
+        out[start:start + ref.shape[0], :] = place
+
+
+def kernel(count, rows, slots, kept, x_hbm, cols_ref, kept_ref, sq_out, new_out, x_ref, tab, found,
+           own_f, a, d, sq, new, send_sem, recv_sem, out_sem, in_sem, *bufs):
     width = x_ref.shape[-1]
+    load_x = pltpu.make_async_copy(x_hbm, x_ref, in_sem.at[0])
+    load_x.start()
     span = LAYERS * rows
     pairs = rows // 2
     me = lax.axis_index("row")
@@ -62,9 +71,8 @@
         pl.semaphore_signal(barrier, inc=1, device_id={"row": other}, device_id_type=MESH)
     pl.semaphore_wait(barrier, 4)
 
-    slots_at = (0, span * span)
-    kept_at = 2 * span * span
-    cols_at = kept_at + rows * kept
+    starts = table_rows(span, slots, kept)
+    layers = window_layers(me, count)
     depth = (slots, kept)
     pieces = rows * HALVES
 
@@ -87,7 +95,7 @@
     def own_piece(stage, piece):
         row, half = piece // HALVES, piece % HALVES
         length = depth[stage] // HALVES
-        ref = (x_ref, own_f)[stage]
+        ref = (x_hbm, own_f)[stage]
         return ref.at[row, pl.ds(half * length, length)]
 
     def to_mate(stage, piece):
@@ -118,14 +126,13 @@
             ref, base = (x_ref, own_f)[stage], 2 * pair
         else:
             ref, base = bufs[(stage * 4 + source - 1) * pairs + pair], 0
-        line = slots_at[stage] + (source * rows + 2 * pair) * span
+        line = layers[source] * rows + 2 * pair
 
         def body(step, carry):
             lines = []
             for row in range(2):
-                at = line + row * span + 2 * step
                 lines.append(jnp.concatenate(
-                    [block(ref, base + row, tab[at]), block(ref, base + row, tab[at + 1])], axis=1))
+                    [block(ref, base + row, tab[starts[stage] + 2 * step + col, line + row]) for col in range(2)], axis=1))
             right = jnp.concatenate(lines, axis=0)
             part = jnp.dot(a[source * pairs + pair], right, preferred_element_type=jnp.float32)
             for col in range(2):
@@ -136,7 +143,7 @@
                     d[2 * step + col] += piece
             return carry
 
-        lax.fori_loop(0, span // 2, body, 0)
+        lax.fori_loop(0, span // 2, body, 0, unroll=10)
 
     def gather_and_multiply(stage):
         for pair in range(pairs):
@@ -175,11 +182,16 @@
 
     for row in range(rows):
         start_own(0, row)
+    fill_tables(cols_ref, kept_ref, found, layers, rows, starts)
+    load_tab = pltpu.make_async_copy(found, tab, in_sem.at[1])
+    load_tab.start()
+    load_tab.wait()
+    load_x.wait()
 
     def build(step, carry):
         for row in range(rows):
             for col in range(2):
-                slot = tab[row * span + 2 * step + col]
+                slot = tab[2 * step + col, me * rows + row]
                 a[step, row * width:(row + 1) * width, col * width:(col + 1) * width] = block(
                     x_ref, row, slot)
         return carry
@@ -191,7 +203,7 @@
            == lax.broadcasted_iota(jnp.int32, (width, width), 1)).astype(jnp.float32)
     for row in range(rows):
         def pick(slot, carry):
-            place = tab[kept_at + row * kept + slot]
+            place = tab[starts[2] + slot, me * rows + row]
             value = d[place, row * width:(row + 1) * width, :]
             sq[row, slot] = value
             three = jnp.where(place == row, 3.0, 0.0)
@@ -206,7 +218,7 @@
 
     for row in range(rows):
         def pick(slot, carry):
-            place = tab[cols_at + row * slots + slot]
+            place = tab[starts[3] + slot, me * rows + row]
             new[row, slot] = 0.5 * d[place, row * width:(row + 1) * width, :]
             return carry
 
@@ -227,8 +239,6 @@
 def local(count, blocks, block_cols, kept_cols):
     rows, slots, width, _ = blocks.shape
     kept = kept_cols.shape[1]
-    me = lax.axis_index("row")
-    table = tables(block_cols, kept_cols, me, count, rows)
     span = LAYERS * rows
     pieces = rows * HALVES
     landings = [
@@ -242,9 +252,12 @@
             jax.ShapeDtypeStruct((rows, kept, width, width), jnp.float32),
             jax.ShapeDtypeStruct((rows, slots, width, width), jnp.float32),
         ),
-        in_specs=[pl.BlockSpec(memory_space=pltpu.VMEM), pl.BlockSpec(memory_space=pltpu.SMEM)],
+        in_specs=[pl.BlockSpec(memory_space=pl.ANY)] + [pl.BlockSpec(memory_space=pltpu.VMEM)] * 2,
         out_specs=(pl.BlockSpec(memory_space=pl.ANY), pl.BlockSpec(memory_space=pl.ANY)),
         scratch_shapes=[
+            pltpu.VMEM((rows, slots, width, width), jnp.bfloat16),
+            pltpu.SMEM((table_rows(span, slots, kept)[-1], block_cols.shape[0]), jnp.int32),
+            pltpu.VMEM((table_rows(span, slots, kept)[-1], block_cols.shape[0]), jnp.int32),
             pltpu.VMEM((rows, kept, width, width), jnp.bfloat16),
             pltpu.VMEM((LAYERS * rows // 2, rows * width, 2 * width), jnp.bfloat16),
             pltpu.VMEM((span, rows * width, width), jnp.float32),
@@ -253,11 +266,12 @@
             pltpu.SemaphoreType.DMA((2, 4, pieces)),
             pltpu.SemaphoreType.DMA((2, 4, pieces)),
             pltpu.SemaphoreType.DMA((2, rows)),
+            pltpu.SemaphoreType.DMA((2,)),
         ] + landings,
         compiler_params=pltpu.CompilerParams(
-            collective_id=0, has_side_effects=True, vmem_limit_bytes=48 * 1024 * 1024
+            collective_id=0, has_side_effects=True, vmem_limit_bytes=60 * 1024 * 1024
         ),
-    )(blocks, table)
+    )(blocks, block_cols.T, kept_cols.T)
 
 
 def solution(mesh):

time: 133 us -> 118 us (0.89)
  Pallas kernels: 118 us -> 110 us
  local copies, waits for them, and re-layouts: 11 us -> 6.29 us
    pallas_call x1, Pallas kernels: 118 us -> 110 us  [local(): pl.pallas_call(functools.partial(kernel, count, rows, slots, kept), out_s...]
    unnamed x8 -> x4, local copies, waits for them, and re-layouts: 8.28 us -> 6.29 us
where the time goes in v2:
time: 118 us; the launch traced here: 117 us
  Pallas kernels  110 us (93%)
  local copies, waits for them, and re-layouts  6.29 us (5%)
    pallas_call x1, Pallas kernels, local(): pl.pallas_call(functools.partial(kernel, count, rows, slots, kept), out_s...  110 us
    unnamed x4, local copies, waits for them, and re-layouts  6.29 us

profile of v2, /device:TPU:1, one launch (start us, length us, event | category | flops | bytes accessed | tf_op | source)
XLA Modules:
  0.0 116.6 jit_solution(2547817671333784830)
XLA Ops:
  0.6 109.6 %shard_map.50 = (f32[4,14,128,128]{3,2,1,0:T(8,128)}, f32[4,14,128,128]{3,2,1,0:T(8,128)}) custom-call(bf16[4,14,128,128]{3,2,1,0:T(8,128)(2,1)} %x_hbm.1, s32[14,64]{1,0:T(8,128)} %bitcast.2, s32[14,64]{1,0:T(8,128)} %bitcast.3), custom_call_target="tpu_custom_call" | custom-call | tf_op jit(solution)/shard_map/pallas_call | solution.py:249
  110.3 0.0 copy-start
  110.3 4.5 %copy.7 = f32[4,14,128,128]{3,2,1,0:T(8,128)} copy(f32[4,14,128,128]{3,2,1,0:T(8,128)} %get-tuple-element.4) | data formatting | bytes 7340032
  114.7 0.0 copy-done
  114.7 1.8 %copy.8 = f32[4,14,128,128]{3,2,1,0:T(8,128)} copy(f32[4,14,128,128]{3,2,1,0:T(8,128)S(1)} %copy-done) | data formatting | bytes 7340032
Async XLA Ops:
  110.3 4.5 %copy-start = (f32[4,14,128,128]{3,2,1,0:T(8,128)S(1)}, f32[4,14,128,128]{3,2,1,0:T(8,128)}, u32[]{:S(2)}) copy-start(f32[4,14,128,128]{3,2,1,0:T(8,128)} %get-tuple-element.5) | copy-start | bytes 11010052

commit v3 on v2

v3 whole, which is shorter than its diff:
```python
import functools

import jax
import jax.numpy as jnp
from jax import lax
from jax.experimental import pallas as pl
from jax.experimental.pallas import tpu as pltpu
from jax.sharding import PartitionSpec as P

MESH = pl.DeviceIdType.MESH
LAYERS = 5
HALVES = 2


def window_layers(me, count):
    core, side = me % 2, (me // 2) % 2
    away = jnp.where(side == 0, 1, -1)
    return [
        me,
        me + 1 - 2 * core,
        (me + 2 * away + count) % count,
        (me - 2 * away + count) % count,
        (me - 1 + 2 * core + count) % count,
    ]


def table_rows(span, slots, kept):
    starts = [0]
    for length in (span, span, kept, slots):
        starts.append(starts[-1] + (length + 7) // 8 * 8)
    return starts


def fill_tables(cols_ref, kept_ref, out, layers, rows, starts):
    span = LAYERS * rows
    line = lax.broadcasted_iota(jnp.int32, (span, cols_ref.shape[1]), 0)
    ids = jnp.zeros_like(line)
    for index, layer in enumerate(layers):
        ids = jnp.where(line // rows == index, layer * rows + line % rows, ids)
    for start, ref in zip(starts[:2], (cols_ref, kept_ref)):
        found = jnp.full_like(ids, -1)
        for slot in range(ref.shape[0]):
            found = jnp.where(ref[slot:slot + 1, :] == ids, slot, found)
        out[start:start + span, :] = found
    for start, ref in zip(starts[2:4], (kept_ref, cols_ref)):
        cols = ref[...]
        place = jnp.zeros_like(cols)
        for index, layer in enumerate(layers):
            for row in range(rows):
                place = jnp.where(cols == layer * rows + row, index * rows + row, place)
        out[start:start + ref.shape[0], :] = place


def kernel(count, rows, slots, kept, x_hbm, cols_ref, kept_ref, sq_out, new_out, x_ref, tab, found,
           a, d, sq, new, send_sem, recv_sem, out_sem, in_sem, *bufs):
    width = x_ref.shape[-1]
    part_width = width // HALVES
    load_x = pltpu.make_async_copy(x_hbm, x_ref, in_sem.at[0])
    load_x.start()
    span = LAYERS * rows
    pairs = rows // 2
    me = lax.axis_index("row")
    core, side = me % 2, (me // 2) % 2
    mate = me + 1 - 2 * core
    across = me + 2 - 4 * side
    onward = (me + 4 - 8 * side + count) % count
    behind = (me - 4 + 8 * side + count) % count
    shares_first = core == side
    own, bufs = bufs[:2 * HALVES], bufs[2 * HALVES:]

    barrier = pltpu.get_barrier_semaphore()
    for other in (mate, across, onward, behind):
        pl.semaphore_signal(barrier, inc=1, device_id={"row": other}, device_id_type=MESH)
    pl.semaphore_wait(barrier, 4)

    starts = table_rows(span, slots, kept)
    layers = window_layers(me, count)
    pieces = rows * HALVES

    def landed(source, piece):
        return bufs[(piece // 2) * 4 + source]

    def landing(source, piece):
        return landed(source, piece).at[piece % 2]

    def copy(source, piece, src, device):
        return pltpu.make_async_remote_copy(
            src_ref=src,
            dst_ref=landing(source, piece),
            send_sem=send_sem.at[source, piece],
            recv_sem=recv_sem.at[source, piece],
            device_id={"row": device},
            device_id_type=MESH,
        )

    def own_piece(piece):
        return own[piece // rows].at[piece % rows]

    def to_mate(piece):
        return copy(0, piece, own_piece(piece), mate)

    def to_across(piece):
        return copy(1, piece, own_piece(piece), across)

    def to_onward(piece):
        return copy(2, piece, landing(1, piece), onward)

    def share(piece, source):
        return copy(3, piece, landing(source, piece), mate)

    def block(ref, row, slot):
        value = ref[row, jnp.maximum(slot, 0)]
        return jnp.where(slot >= 0, value, jnp.zeros_like(value))

    def multiply(phase, source, pair):
        stage, half = phase // HALVES, phase % HALVES
        first = source == 0 and pair == 0
        if source == 0:
            ref, base = own[phase], 2 * pair
        else:
            ref, base = bufs[(phase * pairs + pair) * 4 + source - 1], 0
        line = layers[source] * rows + 2 * pair
        group = span // 2

        def body(step, carry):
            left = jnp.concatenate([
                jnp.concatenate(
                    [block(ref, base + row, tab[starts[stage] + group * step + col, line + row])
                     for row in range(2)], axis=1)
                for col in range(group)], axis=0)
            part = jnp.dot(left, a[source * pairs + pair], preferred_element_type=jnp.float32)
            for col in range(group):
                piece = part[col * part_width:(col + 1) * part_width]
                if first:
                    d[half, group * step + col] = piece
                else:
                    d[half, group * step + col] += piece
            return carry

        lax.fori_loop(0, 2, body, 0)

    def near(phase):
        for pair in range(pairs):
            multiply(phase, 0, pair)
        for piece in range(phase * rows, (phase + 1) * rows):
            to_mate(piece).wait_recv()
        for pair in range(pairs):
            multiply(phase, 1, pair)

    def finish(phase):
        stage, half = phase // HALVES, phase % HALVES
        for row in range(rows):
            lanes = pl.ds(row * width, width)
            columns = pl.ds(half * part_width, part_width)
            if stage == 0:
                line = lax.broadcasted_iota(jnp.int32, (part_width, width), 0) + half * part_width
                eye = (line == lax.broadcasted_iota(jnp.int32, (part_width, width), 1)).astype(
                    jnp.float32)

                def pick(slot, carry):
                    place = tab[starts[2] + slot, me * rows + row]
                    value = d[half, place, :, lanes]
                    sq[row, slot, :, columns] = value.T
                    three = jnp.where(place == row, 3.0, 0.0)
                    own[HALVES + half][row, slot] = (three * eye - value).astype(jnp.bfloat16)
                    return carry

                lax.fori_loop(0, kept, pick, 0)
                piece = pieces + half * rows + row
                to_across(piece).start()
                to_mate(piece).start()
                if half == HALVES - 1:
                    pltpu.make_async_copy(sq.at[row], sq_out.at[row], out_sem.at[0, row]).start()
            else:
                def pick(slot, carry):
                    place = tab[starts[3] + slot, me * rows + row]
                    new[row, slot, :, columns] = 0.5 * d[half, place, :, lanes].T
                    return carry

                lax.fori_loop(0, slots, pick, 0)
                if half == HALVES - 1:
                    pltpu.make_async_copy(new.at[row], new_out.at[row], out_sem.at[1, row]).start()

    load_x.wait()
    for half in range(HALVES):
        for row in range(rows):
            def turn(slot, carry):
                own[half][row, slot] = x_ref[row, slot].T[half * part_width:(half + 1) * part_width]
                return carry

            lax.fori_loop(0, slots, turn, 0)
            to_across(half * rows + row).start()
            to_mate(half * rows + row).start()

    fill_tables(cols_ref, kept_ref, found, layers, rows, starts)
    load_tab = pltpu.make_async_copy(found, tab, in_sem.at[1])
    load_tab.start()
    load_tab.wait()

    def build(step, carry):
        for row in range(rows):
            for col in range(2):
                slot = tab[2 * step + col, layers[0] * rows + row]
                for half in range(HALVES):
                    at = col * width + half * part_width
                    a[step, at:at + part_width, row * width:(row + 1) * width] = block(
                        own[half], row, slot)
        return carry

    lax.fori_loop(0, LAYERS * pairs, build, 0)
    near(0)
    near(1)

    lag = 2
    total = 2 * pieces
    for step in range(total + lag):
        if step < total:
            to_across(step).wait_recv()
            to_onward(step).start()

            @pl.when(shares_first)
            def _():
                share(step, 1).start()

        late = step - lag
        if late >= 0:
            to_onward(late).wait_recv()

            @pl.when(jnp.logical_not(shares_first))
            def _():
                share(late, 2).start()

        if step < total and step % 2 == 1:
            multiply(step // rows, 2, step % rows // 2)
        if late >= 0 and late % 2 == 1:
            phase, pair = late // rows, late % rows // 2
            multiply(phase, 3, pair)
            for piece in (late - 1, late):
                share(piece, 1).wait_recv()
            multiply(phase, 4, pair)
            if pair == pairs - 1:
                finish(phase)
                if phase + HALVES < 2 * HALVES:
                    near(phase + HALVES)

    for piece in range(total):
        to_mate(piece).wait_send()
        to_across(piece).wait_send()
        to_onward(piece).wait_send()
        share(piece, 1).wait_send()
    for row in range(rows):
        pltpu.make_async_copy(sq.at[row], sq_out.at[row], out_sem.at[0, row]).wait()
        pltpu.make_async_copy(new.at[row], new_out.at[row], out_sem.at[1, row]).wait()


def local(count, blocks, block_cols, kept_cols):
    rows, slots, width, _ = blocks.shape
    kept = kept_cols.shape[1]
    span = LAYERS * rows
    pieces = rows * HALVES
    half_width = width // HALVES
    own = [
        pltpu.VMEM((rows, depth, half_width, width), jnp.bfloat16)
        for depth in (slots, kept)
        for _ in range(HALVES)
    ]
    landings = [
        pltpu.VMEM((2, depth, half_width, width), jnp.bfloat16)
        for depth in (slots, kept)
        for _ in range(HALVES * 4 * (rows // 2))
    ]
    return pl.pallas_call(
        functools.partial(kernel, count, rows, slots, kept),
        out_shape=(
            jax.ShapeDtypeStruct((rows, kept, width, width), jnp.float32),
            jax.ShapeDtypeStruct((rows, slots, width, width), jnp.float32),
        ),
        in_specs=[pl.BlockSpec(memory_space=pl.ANY)] + [pl.BlockSpec(memory_space=pltpu.VMEM)] * 2,
        out_specs=(pl.BlockSpec(memory_space=pl.ANY), pl.BlockSpec(memory_space=pl.ANY)),
        scratch_shapes=[
            pltpu.VMEM((rows, slots, width, width), jnp.bfloat16),
            pltpu.SMEM((table_rows(span, slots, kept)[-1], block_cols.shape[0]), jnp.int32),
            pltpu.VMEM((table_rows(span, slots, kept)[-1], block_cols.shape[0]), jnp.int32),
            pltpu.VMEM((LAYERS * rows // 2, 2 * width, rows * width), jnp.bfloat16),
            pltpu.VMEM((HALVES, span, half_width, rows * width), jnp.float32),
            pltpu.VMEM((rows, kept, width, width), jnp.float32),
            pltpu.VMEM((rows, slots, width, width), jnp.float32),
            pltpu.SemaphoreType.DMA((4, 2 * pieces)),
            pltpu.SemaphoreType.DMA((4, 2 * pieces)),
            pltpu.SemaphoreType.DMA((2, rows)),
            pltpu.SemaphoreType.DMA((2,)),
        ] + own + landings,
        compiler_params=pltpu.CompilerParams(
            collective_id=0, has_side_effects=True, vmem_limit_bytes=60 * 1024 * 1024
        ),
    )(blocks, block_cols.T, kept_cols.T)


def solution(mesh):
    count = mesh.shape["row"]
    in_specs = (P(("groups", "row"), None, None, None), P("groups", None), P("groups", None))
    out_specs = (P(("groups", "row"), None, None, None), P(("groups", "row"), None, None, None))
    return jax.shard_map(
        functools.partial(local, count), mesh=mesh, in_specs=in_specs, out_specs=out_specs,
        check_vma=False)
```

time: 118 us -> 132 us (1.12)
  Pallas kernels: 110 us -> 123 us
    pallas_call x1, Pallas kernels: 110 us -> 123 us  [local(): pl.pallas_call(functools.partial(kernel, count, rows, slots, kept), out_s...]
where the time goes in v3:
time: 132 us; the launch traced here: 129 us
  Pallas kernels  123 us (93%)
  local copies, waits for them, and re-layouts  6.29 us (5%)
    pallas_call x1, Pallas kernels, local(): pl.pallas_call(functools.partial(kernel, count, rows, slots, kept), out_s...  123 us
    unnamed x4, local copies, waits for them, and re-layouts  6.29 us

profile of v3, /device:TPU:1, one launch (start us, length us, event | category | flops | bytes accessed | tf_op | source)
XLA Modules:
  0.0 129.5 jit_solution(11421751701806071608)
XLA Ops:
  0.6 122.6 %shard_map.50 = (f32[4,14,128,128]{3,2,1,0:T(8,128)}, f32[4,14,128,128]{3,2,1,0:T(8,128)}) custom-call(bf16[4,14,128,128]{3,2,1,0:T(8,128)(2,1)} %x_hbm.1, s32[14,64]{1,0:T(8,128)} %bitcast.2, s32[14,64]{1,0:T(8,128)} %bitcast.3), custom_call_target="tpu_custom_call" | custom-call | tf_op jit(solution)/shard_map/pallas_call | solution.py:272
  123.2 0.0 copy-start
  123.2 4.5 %copy.7 = f32[4,14,128,128]{3,2,1,0:T(8,128)} copy(f32[4,14,128,128]{3,2,1,0:T(8,128)} %get-tuple-element.4) | data formatting | bytes 7340032
  127.7 0.0 copy-done
  127.7 1.8 %copy.8 = f32[4,14,128,128]{3,2,1,0:T(8,128)} copy(f32[4,14,128,128]{3,2,1,0:T(8,128)S(1)} %copy-done) | data formatting | bytes 7340032
Async XLA Ops:
  123.2 4.5 %copy-start = (f32[4,14,128,128]{3,2,1,0:T(8,128)S(1)}, f32[4,14,128,128]{3,2,1,0:T(8,128)}, u32[]{:S(2)}) copy-start(f32[4,14,128,128]{3,2,1,0:T(8,128)} %get-tuple-element.5) | copy-start | bytes 11010052

commit v4 on v3

--- a/solution.py
+++ b/solution.py
@@ -137,7 +137,7 @@
                     d[half, group * step + col] += piece
             return carry
 
-        lax.fori_loop(0, 2, body, 0)
+        lax.fori_loop(0, 2, body, 0, unroll=True)
 
     def near(phase):
         for pair in range(pairs):
@@ -165,7 +165,7 @@
                     own[HALVES + half][row, slot] = (three * eye - value).astype(jnp.bfloat16)
                     return carry
 
-                lax.fori_loop(0, kept, pick, 0)
+                lax.fori_loop(0, kept, pick, 0, unroll=7)
                 piece = pieces + half * rows + row
                 to_across(piece).start()
                 to_mate(piece).start()
@@ -177,7 +177,7 @@
                     new[row, slot, :, columns] = 0.5 * d[half, place, :, lanes].T
                     return carry
 
-                lax.fori_loop(0, slots, pick, 0)
+                lax.fori_loop(0, slots, pick, 0, unroll=7)
                 if half == HALVES - 1:
                     pltpu.make_async_copy(new.at[row], new_out.at[row], out_sem.at[1, row]).start()
 
@@ -188,7 +188,7 @@
                 own[half][row, slot] = x_ref[row, slot].T[half * part_width:(half + 1) * part_width]
                 return carry
 
-            lax.fori_loop(0, slots, turn, 0)
+            lax.fori_loop(0, slots, turn, 0, unroll=7)
             to_across(half * rows + row).start()
             to_mate(half * rows + row).start()
 

time: 132 us -> 110 us (0.83); the launches traced: 129 us -> 109 us
  Pallas kernels: 123 us -> 102 us
    pallas_call x1, Pallas kernels: 123 us -> 102 us  [local(): pl.pallas_call(functools.partial(kernel, count, rows, slots, kept), out_s...]
where the time goes in v4:
time: 110 us; the launch traced here: 109 us
  Pallas kernels  102 us (93%)
  local copies, waits for them, and re-layouts  6.29 us (6%)
    pallas_call x1, Pallas kernels, local(): pl.pallas_call(functools.partial(kernel, count, rows, slots, kept), out_s...  102 us
    unnamed x4, local copies, waits for them, and re-layouts  6.29 us

profile of v4, /device:TPU:1, one launch (start us, length us, event | category | flops | bytes accessed | tf_op | source)
XLA Modules:
  0.0 108.9 jit_solution(16523268321637946386)
XLA Ops:
  0.6 102.0 %shard_map.50 = (f32[4,14,128,128]{3,2,1,0:T(8,128)}, f32[4,14,128,128]{3,2,1,0:T(8,128)}) custom-call(bf16[4,14,128,128]{3,2,1,0:T(8,128)(2,1)} %x_hbm.1, s32[14,64]{1,0:T(8,128)} %bitcast.2, s32[14,64]{1,0:T(8,128)} %bitcast.3), custom_call_target="tpu_custom_call" | custom-call | tf_op jit(solution)/shard_map/pallas_call | solution.py:272
  102.6 0.0 copy-start
  102.6 4.5 %copy.7 = f32[4,14,128,128]{3,2,1,0:T(8,128)} copy(f32[4,14,128,128]{3,2,1,0:T(8,128)} %get-tuple-element.4) | data formatting | bytes 7340032
  107.1 0.0 copy-done
  107.1 1.8 %copy.8 = f32[4,14,128,128]{3,2,1,0:T(8,128)} copy(f32[4,14,128,128]{3,2,1,0:T(8,128)S(1)} %copy-done) | data formatting | bytes 7340032
Async XLA Ops:
  102.6 4.5 %copy-start = (f32[4,14,128,128]{3,2,1,0:T(8,128)S(1)}, f32[4,14,128,128]{3,2,1,0:T(8,128)}, u32[]{:S(2)}) copy-start(f32[4,14,128,128]{3,2,1,0:T(8,128)} %get-tuple-element.5) | copy-start | bytes 11010052
